TPU v7x, 256 devices: a whole 4x4x8 slice. The times are simulated.
256 devices in a mesh: tok: 8 (over y, z_hi), hid: 32 (over z_lo, x, core).
Axes of the slice: x: 4, y: 4, z: 8 (z_hi: 2, z_lo: 4; z = z_hi * 4 + z_lo), core: 2. Of those that a mesh axis runs over, the one named last changes fastest.
Arguments:
- student_in: bfloat16 [1024, 8192], P('hid', 'tok'), may hold values from -6 to 6
- target_delta: bfloat16 [1024, 8192], P('hid', 'tok'), may hold values from -3 to 3
- gate_weight: bfloat16 [8192, 16384], P('tok', 'hid'), may hold values from -0.0625 to 0.0625
- up_weight: bfloat16 [8192, 16384], P('tok', 'hid'), may hold values from -0.0625 to 0.0625
- down_weight: bfloat16 [16384, 8192], P('hid', 'tok'), may hold values from -0.046875 to 0.046875
- block_mask: int32 [3, 64, 128], P(None, 'tok', 'hid'), may hold values from 0 to 1, as said below
Outputs:
- student_out: bfloat16 [1024, 8192], P('hid', 'tok')
- input_grad: bfloat16 [1024, 8192], P('hid', 'tok')
- gate_wgrad: float32 [8192, 16384], P('tok', 'hid')
- up_wgrad: float32 [8192, 16384], P('tok', 'hid')
- down_wgrad: float32 [16384, 8192], P('hid', 'tok')
Inputs may be any that keep to these rules, and one draw needn't show every extreme that they name: `block_mask`: each entry is 0 or 1 (1 keeps a 128 x 128 block of weights); the share of ones differs from one block column of hidden units to another.
All inputs are finite; a program needn't handle non-finite values.
Results may differ from a plain program's by a relative error of at most 0.0056.
Values may be sent and summed in bfloat16 or wider, within the bound.
A program may use at most 64 MiB of HBM per device.

v0:
```python
import jax
import jax.numpy as jnp
from jax import lax
from jax.sharding import PartitionSpec as P

BLOCK = 128


def widen(blocks):
    return jnp.repeat(jnp.repeat(blocks, BLOCK, axis=0), BLOCK, axis=1)


def per_device(student_in, target_delta, gate_weight, up_weight, down_weight, block_mask):
    by_cols = (((1,), (1,)), ((), ()))
    by_rows = (((0,), (0,)), ((), ()))
    gate_mask = widen(block_mask[0]).astype(jnp.bfloat16)
    up_mask = widen(block_mask[1]).astype(jnp.bfloat16)
    down_mask = widen(block_mask[2]).T.astype(jnp.bfloat16)
    gate_eff = gate_weight * gate_mask
    up_eff = up_weight * up_mask
    down_eff = down_weight * down_mask
    hidden_cols = gate_weight.shape[1]
    rows_end = student_in.shape[0]
    total_rows = rows_end * lax.axis_size("hid")
    factor = 1.0 / jnp.sqrt(jnp.float32(total_rows))
    inputs_all = lax.all_gather(student_in, "hid", axis=0, tiled=True)
    piece = inputs_all
    gate_part = jnp.dot(piece, gate_eff, preferred_element_type=jnp.float32)
    up_part = jnp.dot(piece, up_eff, preferred_element_type=jnp.float32)
    both = lax.psum_scatter(
        jnp.concatenate([gate_part, up_part], axis=1), "tok", scatter_dimension=0, tiled=True
    )
    gate = both[:, :hidden_cols]
    up = both[:, hidden_cols:]
    sigma = jax.nn.sigmoid(gate)
    swish = gate * sigma
    hidden = (swish * up).astype(jnp.bfloat16)
    hidden_all = lax.all_gather(hidden, "tok", axis=0, tiled=True)
    piece = hidden_all
    output_sum = lax.psum_scatter(
        jnp.dot(piece, down_eff, preferred_element_type=jnp.float32),
        "hid",
        scatter_dimension=0,
        tiled=True,
    )
    error = (output_sum - target_delta.astype(jnp.float32)).astype(jnp.bfloat16)
    error_all = lax.all_gather(error, "hid", axis=0, tiled=True)
    piece = error_all
    hidden_grad = lax.psum_scatter(
        lax.dot_general(piece, down_eff, by_cols, preferred_element_type=jnp.float32),
        "tok",
        scatter_dimension=0,
        tiled=True,
    )
    gate_grad = (hidden_grad * up * (sigma + gate * sigma * (1.0 - sigma))).astype(jnp.bfloat16)
    up_grad = (hidden_grad * swish).astype(jnp.bfloat16)
    gate_grad_all, up_grad_all = (
        lax.all_gather(gate_grad, "tok", axis=0, tiled=True),
        lax.all_gather(up_grad, "tok", axis=0, tiled=True),
    )
    gate_wgrad = (
        lax.dot_general(inputs_all, gate_grad_all, by_rows, preferred_element_type=jnp.float32)
        * gate_mask.astype(jnp.float32)
        * factor
    )
    up_wgrad = (
        lax.dot_general(inputs_all, up_grad_all, by_rows, preferred_element_type=jnp.float32)
        * up_mask.astype(jnp.float32)
        * factor
    )
    down_wgrad = (
        lax.dot_general(hidden_all, error_all, by_rows, preferred_element_type=jnp.float32)
        * down_mask.astype(jnp.float32)
        * factor
    )
    first = lax.dot_general(gate_grad_all, gate_eff, by_cols, preferred_element_type=jnp.float32)
    input_grad = lax.psum_scatter(
        first + lax.dot_general(up_grad_all, up_eff, by_cols, preferred_element_type=jnp.float32),
        "hid",
        scatter_dimension=0,
        tiled=True,
    ).astype(jnp.bfloat16)
    return (output_sum.astype(jnp.bfloat16), input_grad, gate_wgrad, up_wgrad, down_wgrad)


def solution(mesh):
    placed = (
        P("hid", "tok"),
        P("hid", "tok"),
        P("tok", "hid"),
        P("tok", "hid"),
        P("hid", "tok"),
        P(None, "tok", "hid"),
    )
    return jax.shard_map(
        per_device,
        mesh=mesh,
        in_specs=placed,
        out_specs=(
            P("hid", "tok"),
            P("hid", "tok"),
            P("tok", "hid"),
            P("tok", "hid"),
            P("hid", "tok"),
        ),
        check_vma=False,
    )
```

profile of v0, /device:TPU:1, one launch (start us, length us, event | category | flops | bytes accessed | tf_op | source)
XLA Modules:
  0.0 852.3 jit_solution(9813071012821765858)
XLA Ops:
  10.4 63.9 %all-gather.6.cloned.1.call-done = bf16[1024,1024]{1,0:T(8,128)(2,1)} async-done(((bf16[32,1024]{1,0:T(8,128)(2,1)}), bf16[1024,1024]{1,0:T(8,128)(2,1)}) %all-gather.6.cloned.1.call-update) | async-done | bytes 2097168 | tf_op jit(solution)/shard_map/all_gather | solution.py:26
  74.3 3.0 convolution_bitcast_fusion
  78.6 2.5 pad_maximum_fusion
  81.2 124.3 %reduce-scatter.5.cloned.1.call-done = f32[128,1024]{0,1:T(8,128)} async-done(((f32[1024,1024]{0,1:T(8,128)}), f32[128,1024]{0,1:T(8,128)}) %reduce-scatter.5.cloned.1.call-update) | async-done | bytes 524304 | tf_op jit(solution)/shard_map/reduce_scatter | solution.py:30
  205.5 1.8 multiply_convert_fusion.2
  208.6 57.1 %all-gather.8.cloned.1.call-done = bf16[1024,512]{0,1:T(8,128)(2,1)} async-done(((bf16[128,512]{0,1:T(8,128)(2,1)}), bf16[1024,512]{0,1:T(8,128)(2,1)}) %all-gather.8.cloned.1.call-update) | async-done | bytes 1048592 | tf_op jit(solution)/shard_map/all_gather | solution.py:38
  265.7 4.5 fusion.2
  270.2 142.4 %reduce-scatter.7.cloned.1.call-done = f32[32,1024]{1,0:T(8,128)} async-done(((f32[1024,1024]{1,0:T(8,128)}), f32[32,1024]{1,0:T(8,128)}) %reduce-scatter.7.cloned.1.call-update) | async-done | bytes 131088 | tf_op jit(solution)/shard_map/reduce_scatter | solution.py:40
  412.6 1.7 subtract_convert_fusion
  414.3 62.7 %all-gather.10.cloned.1.call-done = bf16[1024,1024]{1,0:T(8,128)(2,1)} async-done(((bf16[32,1024]{1,0:T(8,128)(2,1)}), bf16[1024,1024]{1,0:T(8,128)(2,1)}) %all-gather.10.cloned.1.call-update) | async-done | bytes 2097168 | tf_op jit(solution)/shard_map/all_gather | solution.py:47
  477.0 4.2 fusion.3
  481.3 93.1 %reduce-scatter.9.cloned.1.call-done = f32[128,512]{0,1:T(8,128)} async-done(((f32[1024,512]{0,1:T(8,128)}), f32[128,512]{0,1:T(8,128)}) %reduce-scatter.9.cloned.1.call-update) | async-done | bytes 262160 | tf_op jit(solution)/shard_map/reduce_scatter | solution.py:49
  574.3 1.8 multiply_convert_fusion
  577.1 58.0 %all-gather.12.cloned.1.call-done = bf16[1024,512]{0,1:T(8,128)(2,1)} async-done(((bf16[128,512]{0,1:T(8,128)(2,1)}), bf16[1024,512]{0,1:T(8,128)(2,1)}) %all-gather.12.cloned.1.call-update) | async-done | bytes 1048592 | tf_op jit(solution)/shard_map/all_gather | solution.py:58
  635.1 4.5 fusion.4
  639.6 56.3 %all-gather.14.cloned.1.call-done = bf16[1024,512]{0,1:T(8,128)(2,1)} async-done(((bf16[128,512]{0,1:T(8,128)(2,1)}), bf16[1024,512]{0,1:T(8,128)(2,1)}) %all-gather.14.cloned.1.call-update) | async-done | bytes 1048592 | tf_op jit(solution)/shard_map/all_gather | solution.py:59
  695.9 5.8 convolution_add_fusion
  702.9 4.3 multiply_multiply_fusion
  707.3 2.6 fusion.1
  709.9 3.0 copy.14
  713.0 4.3 fusion
  717.3 2.9 copy.15
  720.2 124.0 %reduce-scatter.11.cloned.1.call-done = f32[32,1024]{1,0:T(8,128)} async-done(((f32[1024,1024]{1,0:T(8,128)}), f32[32,1024]{1,0:T(8,128)}) %reduce-scatter.11.cloned.1.call-update) | async-done | bytes 131088 | tf_op jit(solution)/shard_map/reduce_scatter | solution.py:77
  844.2 1.5 convert_element_type.85
  (52 shorter events, 8.4 us)
Async XLA Ops:
  7.2 2.3 copy-start.6
  7.2 2.4 copy-start.4
  7.2 67.1 %all-gather.6.cloned.1.call-start = ((), (), s32[]{:S(2)}) async-start(), calls=%async_computation.4 | async-start | bytes 2162688 | tf_op jit(solution)/shard_map/all_gather | solution.py:26
  7.9 197.5 %reduce-scatter.5.cloned.1.call-start = ((), (), s32[]{:S(2)}) async-start(), calls=%async_computation.5 | async-start | bytes 4718592 | tf_op jit(solution)/shard_map/reduce_scatter | solution.py:30
  74.3 3.0 copy-start.7
  81.1 184.5 %all-gather.8.cloned.1.call-start = ((), (), s32[]{:S(2)}) async-start(), calls=%async_computation.6 | async-start | bytes 1179648 | tf_op jit(solution)/shard_map/all_gather | solution.py:38
  207.2 205.4 %reduce-scatter.7.cloned.1.call-start = ((), (), s32[]{:S(2)}) async-start(), calls=%async_computation.7 | async-start | bytes 4325376 | tf_op jit(solution)/shard_map/reduce_scatter | solution.py:40
  270.1 142.5 %copy-start.5 = (bf16[32,1024]{1,0:T(8,128)(2,1)S(1)}, bf16[32,1024]{1,0:T(8,128)(2,1)}, u32[]{:S(2)}) copy-start(bf16[32,1024]{1,0:T(8,128)(2,1)} %param.7) | copy-start | bytes 196612
  270.2 206.9 %all-gather.10.cloned.1.call-start = ((), (), s32[]{:S(2)}) async-start(), calls=%async_computation.8 | async-start | bytes 2162688 | tf_op jit(solution)/shard_map/all_gather | solution.py:47
  414.3 160.1 %reduce-scatter.9.cloned.1.call-start = ((), (), s32[]{:S(2)}) async-start(), calls=%async_computation.9 | async-start | bytes 2359296 | tf_op jit(solution)/shard_map/reduce_scatter | solution.py:49
  481.2 93.1 %copy-start.1 = (f32[128,1024]{0,1:T(8,128)S(1)}, f32[128,1024]{0,1:T(8,128)}, u32[]{:S(2)}) copy-start(f32[128,1024]{0,1:T(8,128)} %reduce-scatter.5.cloned.1.call-done) | copy-start | bytes 1572868
  481.2 153.9 %all-gather.12.cloned.1.call-start = ((), (), s32[]{:S(2)}) async-start(), calls=%async_computation.10 | async-start | bytes 1179648 | tf_op jit(solution)/shard_map/all_gather | solution.py:58
  576.2 119.7 %all-gather.14.cloned.1.call-start = ((), (), s32[]{:S(2)}) async-start(), calls=%async_computation.11 | async-start | bytes 1179648 | tf_op jit(solution)/shard_map/all_gather | solution.py:59
  576.9 267.3 %reduce-scatter.11.cloned.1.call-start = ((), (), s32[]{:S(2)}) async-start(), calls=%async_computation.12 | async-start | bytes 4325376 | tf_op jit(solution)/shard_map/reduce_scatter | solution.py:77
  701.6 1.2 copy-start.2
  702.9 4.4 copy-start.3
  702.9 4.5 copy-start.8
  709.9 3.1 copy-start
Sparse Core Ops, SparseCore 0:
  9.9 64.3 all-gather.5
  81.2 124.1 reduce-scatter.4
  208.5 57.1 all-gather.7
  270.3 142.2 reduce-scatter.6
  414.9 62.0 all-gather.9
  481.5 92.7 reduce-scatter.8
  577.7 57.3 all-gather.11
  638.5 57.3 all-gather.13
  701.8 142.3 reduce-scatter.10
where the time goes:
time: 857 us; the launch traced here: 852 us
  waiting for transfers between devices  783 us (91%)
  matrix products  34.4 us (4%)
  between operations  14 us (2%)
  other arithmetic  10.7 us (1%)
  local copies, waits for them, and re-layouts  9.51 us (1%)
    reduce_scatter x1, waiting for transfers between devices, per_device(): lax.psum_scatter(jnp.dot(piece, down_eff, preferred_element_type=jnp.floa...  142 us
    reduce_scatter x1, waiting for transfers between devices, per_device(): lax.psum_scatter(jnp.concatenate([gate_part, up_part], axis=1), 'tok', sc...  124 us
    reduce_scatter x1, waiting for transfers between devices, per_device(): lax.psum_scatter(first + lax.dot_general(up_grad_all, up_eff, by_cols, pr...  124 us
    reduce_scatter x1, waiting for transfers between devices, per_device(): lax.psum_scatter(lax.dot_general(piece, down_eff, by_cols, preferred_elem...  93.1 us
    all_gather x1, waiting for transfers between devices, per_device(): inputs_all = lax.all_gather(student_in, 'hid', axis=0, tiled=True)  63.9 us
    all_gather x1, waiting for transfers between devices, per_device(): error_all = lax.all_gather(error, 'hid', axis=0, tiled=True)  62.7 us
    all_gather x1, waiting for transfers between devices, per_device(): lax.all_gather(gate_grad, 'tok', axis=0, tiled=True)  58 us
    all_gather x1, waiting for transfers between devices, per_device(): hidden_all = lax.all_gather(hidden, 'tok', axis=0, tiled=True)  57.1 us
  transfers between devices with their start and end apart: 9, of which 9 were waited for; matrix products, arithmetic and copies ran while one was open for 3% of the time, Pallas kernels for 0%

commit v1 on v0

v1 whole, which is shorter than its diff:
```python
import jax
import jax.numpy as jnp
from jax import lax
from jax.experimental import pallas as pl
from jax.experimental.pallas import tpu as pltpu
from jax.sharding import PartitionSpec as P

BF = jnp.bfloat16
F32 = jnp.float32
CHUNKS = 2
LAG = 5
T = 512
R = 16
CHIP = 2 * R
XB = 8 * R
Q = 64
D = 1024
H = 512
COPIES = 220

NN = (((1,), (0,)), ((), ()))
NT = (((1,), (1,)), ((), ()))
TN = (((0,), (0,)), ((), ()))


def mm(a, b, dims):
    return lax.dot_general(a, b, dims, preferred_element_type=F32)


def kernel(
    x_in, t_in, gw, uw, dw, bm,
    out, ig, gwg, uwg, dwg,
    weff, deff, xall, tch, tmp, ps2, own2, yl2, zs2, zl2, gu, hall,
    ss4, sl4, of4, xs4, xl4, zs4, zl4, osw, oland,
    eall, ps6, own6, yl6, zs6, zl6, gall,
    ss8, sl8, of8, xs8, xl8, zs8, zl8, isw, iland,
    wg, dg,
    send_sems, recv_sems, loc_sems,
):
    tok = lax.axis_index("tok")
    hid = lax.axis_index("hid")
    y, zh = lax.div(tok, 2), lax.rem(tok, 2)
    c, x, zl = lax.rem(hid, 2), lax.rem(lax.div(hid, 2), 4), lax.div(hid, 8)

    def dev(y=y, zh=zh, zl=zl, x=x, c=c):
        return {"tok": y * 2 + zh, "hid": (zl * 4 + x) * 2 + c}

    def plus(a, d):
        return lax.rem(a + d, 4)

    sib = dev(c=1 - c)
    xp = [dev(x=plus(x, d)) for d in (1, 2, 3)]
    zp = [dev(zl=plus(zl, d)) for d in (1, 2, 3)]
    yp = [dev(y=plus(y, d)) for d in (1, 2, 3)]
    far = dev(zh=1 - zh)
    peers = [sib, far] + xp + zp + yp

    def rows(start, size):
        return pl.ds(pl.multiple_of(start, 16), size)

    def half(which):
        return pl.ds(pl.multiple_of(which * H, H), H)

    mine, other = half(c), half(1 - c)
    copies = []

    def send(src, dst, device):
        i = len(copies)
        copy = pltpu.make_async_remote_copy(
            src_ref=src, dst_ref=dst, send_sem=send_sems.at[i], recv_sem=recv_sems.at[i],
            device_id=device, device_id_type=pl.DeviceIdType.MESH,
        )
        copy.start()
        copies.append(copy)
        return copy

    def arrived(group):
        for copy in group:
            copy.wait_recv()

    locals_ = []

    def local(src, dst):
        copy = pltpu.make_async_copy(src, dst, loc_sems.at[len(locals_)])
        copy.start()
        locals_.append(copy)
        return copy

    barrier = pltpu.get_barrier_semaphore()
    for peer in peers:
        pl.semaphore_signal(barrier, inc=1, device_id=peer, device_id_type=pl.DeviceIdType.MESH)
    pl.semaphore_wait(barrier, len(peers))

    block = x * XB + zl * CHIP
    first = []
    for k in range(CHUNKS):
        here = xall.at[k, rows(block + c * R, R), mine]
        there = xall.at[k, rows(block + c * R, R), other]
        first.append([send(x_in.at[pl.ds(k * R, R), other], there, sib),
                      local(x_in.at[pl.ds(k * R, R), mine], here)])
    targets = []
    for k in range(CHUNKS):
        spot = tch.at[k, rows(c * R, R)]
        targets.append([send(t_in.at[pl.ds(k * R, R), other], spot, sib),
                        local(t_in.at[pl.ds(k * R, R), mine], spot)])

    def mask_weights():
        @pl.loop(0, 8)
        def _(a):
            at = pl.ds(pl.multiple_of(a * 128, 128), 128)
            for b in range(4):
                lanes = pl.ds(b * 128, 128)
                weff[at, lanes] = (gw[at, lanes].astype(F32) * bm[0, a, b].astype(F32)).astype(BF)
                weff[at, pl.ds(H + b * 128, 128)] = (
                    uw[at, lanes].astype(F32) * bm[1, a, b].astype(F32)
                ).astype(BF)
                deff[lanes, at] = (dw[lanes, at].astype(F32) * bm[2, a, b].astype(F32)).astype(BF)

    def gather_hid(k, buf):
        own = buf.at[k, rows(block, CHIP), mine]
        zc = [send(own, own, p) for p in zp]
        yield
        arrived(zc)
        col = buf.at[k, rows(x * XB, XB), mine]
        xc = [send(col, col, p) for p in xp]
        sc = [send(col, col, sib)]
        for d, xcopy in enumerate(xc):
            yield
            arrived([xcopy])
            got = buf.at[k, rows(plus(x, 3 - d) * XB, XB), mine]
            sc.append(send(got, got, sib))
        yield
        arrived(sc)

    def scatter_tok(k, product, ps, own, yland, zs, zland, width):
        yc = []
        for part in range(2):
            zz = 1 - zh if part == 0 else zh

            @pl.loop(0, width // H)
            def _(n):
                lanes = pl.ds(pl.multiple_of(n * H, H), H)
                value = product(k, zz, lanes)
                tmp[:, lanes] = value
                ps[k, part, :, lanes] = value.astype(BF)

            own[k, part] = tmp[rows(y * Q, Q), pl.ds(0, width)]
            yc.append([send(ps.at[k, part, rows(plus(y, d) * Q, Q)], yland.at[k, part, 3 - d], yp[d - 1])
                       for d in (1, 2, 3)])
        yield
        arrived(yc[0])
        total = own[k, 0]
        for d in range(3):
            total = total + yland[k, 0, d].astype(F32)
        zs[k] = total.astype(zs.dtype)
        zc = send(zs.at[k], zland.at[k], far)
        yield
        arrived(yc[1])
        total = own[k, 1]
        for d in range(3):
            total = total + yland[k, 1, d].astype(F32)
        own[k, 1] = total
        yield
        arrived([zc])

    def gather_tok(k, buf):
        own = buf.at[k, rows(zh * 4 * Q + y * Q, Q)]
        zc = send(own, own, far)
        yc = [send(own, own, p) for p in yp]
        yield
        arrived([zc])
        got = buf.at[k, rows((1 - zh) * 4 * Q + y * Q, Q)]
        yc += [send(got, got, p) for p in yp]
        yield
        arrived(yc)

    def scatter_hid(k, product, ss, sl, of, xs, xl, zs, zland):
        ss[k] = product(k, other).astype(ss.dtype)
        sc = send(ss.at[k], sl.at[k], sib)
        of[k] = product(k, mine)
        yield
        arrived([sc])
        xc = []
        for d in (2, 1, 3):
            at = rows(plus(x, d) * XB, XB)
            xs[k, d - 1] = (of[k, at] + sl[k, at].astype(F32)).astype(BF)
            xc.append(send(xs.at[k, d - 1], xl.at[k, 3 - d], xp[d - 1]))
        at = rows(x * XB, XB)
        of[k, at] = of[k, at] + sl[k, at].astype(F32)
        yield
        arrived(xc)
        total = of[k, at]
        for d in range(3):
            total = total + xl[k, d].astype(F32)
        of[k, at] = total
        zc = []
        for d in (1, 2, 3):
            zs[k, d - 1] = of[k, rows(x * XB + plus(zl, d) * CHIP, CHIP)].astype(BF)
            zc.append(send(zs.at[k, d - 1], zland.at[k, 3 - d], zp[d - 1]))
        yield
        arrived(zc)

    def scattered(k, of, zland):
        total = of[k, rows(block, CHIP)]
        for d in range(3):
            total = total + zland[k, d].astype(F32)
        return total

    def chain(k):
        arrived(first[k][:1])
        first[k][1].wait()
        yield from gather_hid(k, xall)

        def inputs_by_weights(k, zz, lanes):
            return mm(xall[k, rows(zz * 4 * Q, 4 * Q), :], weff[:, lanes], NN)

        yield from scatter_tok(k, inputs_by_weights, ps2, own2, yl2, zs2, zl2, 2 * H)
        gu[k] = own2[k, 1] + zl2[k].astype(F32)
        gate, up = gu[k, :, :H], gu[k, :, H:]
        hall[k, rows(zh * 4 * Q + y * Q, Q), :] = (gate * jax.nn.sigmoid(gate) * up).astype(BF)
        yield from gather_tok(k, hall)

        def hidden_by_down(k, lanes):
            return mm(hall[k], deff[:, lanes], NN)

        yield from scatter_hid(k, hidden_by_down, ss4, sl4, of4, xs4, xl4, zs4, zl4)
        total = scattered(k, of4, zl4)
        arrived(targets[k][:1])
        targets[k][1].wait()
        eall[k, rows(block, CHIP), mine] = (total - tch[k].astype(F32)).astype(BF)
        osw[k] = total.astype(BF)
        out_swap[k] = send(osw.at[k, rows((1 - c) * R, R)], oland.at[k], sib)
        yield from gather_hid(k, eall)

        def error_by_down(k, zz, lanes):
            return mm(eall[k, rows(zz * 4 * Q, 4 * Q), :], deff[...], NT)

        yield from scatter_tok(k, error_by_down, ps6, own6, yl6, zs6, zl6, H)
        hidden_grad = own6[k, 1] + zl6[k].astype(F32)
        gate, up = gu[k, :, :H], gu[k, :, H:]
        sigma = jax.nn.sigmoid(gate)
        at = rows(zh * 4 * Q + y * Q, Q)
        gall[k, at, :H] = (hidden_grad * up * (sigma + gate * sigma * (1.0 - sigma))).astype(BF)
        gall[k, at, H:] = (hidden_grad * (gate * sigma)).astype(BF)
        yield from gather_tok(k, gall)

        def grads_by_weights(k, which):
            return mm(gall[k], weff[which, :], NT)

        yield from scatter_hid(k, grads_by_weights, ss8, sl8, of8, xs8, xl8, zs8, zl8)
        isw[k] = scattered(k, of8, zl8).astype(BF)
        in_swap[k] = send(isw.at[k, rows((1 - c) * R, R)], iland.at[k], sib)

    def scale(which, a, b):
        return bm[which, a, b].astype(F32) * (1.0 / 32.0)

    def weight_grads():
        @pl.loop(0, 2)
        def _(p):
            at = pl.ds(pl.multiple_of(p * 256, 256), 256)
            value = mm(hall[0, :, at], eall[0], TN) + mm(hall[1, :, at], eall[1], TN)
            for i in range(2):
                for a in range(8):
                    dg[pl.ds(pl.multiple_of(p * 256 + i * 128, 128), 128), pl.ds(a * 128, 128)] = (
                        value[i * 128 : i * 128 + 128, a * 128 : a * 128 + 128] * scale(2, a, p * 2 + i)
                    )

        local(dg, dwg)

        @pl.loop(0, 4)
        def _(p):
            at = pl.ds(pl.multiple_of(p * 256, 256), 256)
            value = mm(xall[0, :, at], gall[0], TN) + mm(xall[1, :, at], gall[1], TN)
            for i in range(2):
                for b in range(8):
                    wg[pl.ds(pl.multiple_of(p * 256 + i * 128, 128), 128), pl.ds(b * 128, 128)] = (
                        value[i * 128 : i * 128 + 128, b * 128 : b * 128 + 128]
                        * scale(b // 4, p * 2 + i, b % 4)
                    )

        local(wg.at[:, pl.ds(0, H)], gwg)
        local(wg.at[:, pl.ds(H, H)], uwg)

    out_swap, in_swap = {}, {}
    chains = [chain(k) for k in range(CHUNKS)]
    done = [False] * CHUNKS
    masked = False
    step = 0
    wgrads_at = 10**6
    while not all(done):
        for k in range(CHUNKS):
            if step >= k * LAG and not done[k]:
                done[k] = next(chains[k], True) is True
        if not masked:
            mask_weights()
            masked = True
        step += 1
    weight_grads()
    for k in range(CHUNKS):
        at = pl.ds(k * R, R)
        arrived([out_swap[k], in_swap[k]])
        out[at, mine] = osw[k, rows(c * R, R)]
        out[at, other] = oland[k]
        ig[at, mine] = isw[k, rows(c * R, R)]
        ig[at, other] = iland[k]
    for copy in copies:
        copy.wait_send()
    for copy in locals_[2 * CHUNKS :]:
        copy.wait()


def per_device(student_in, target_delta, gate_weight, up_weight, down_weight, block_mask):
    C = CHUNKS
    vm = pltpu.VMEM

    def scatter_hid_scratch():
        return [
            vm((C, T, H), F32), vm((C, T, H), F32), vm((C, T, H), F32), vm((C, 3, XB, H), BF), vm((C, 3, XB, H), BF),
            vm((C, 3, CHIP, H), BF), vm((C, 3, CHIP, H), BF), vm((C, CHIP, H), BF), vm((C, R, H), BF),
        ]

    def scatter_tok_scratch(width, far_type):
        return [
            vm((C, 2, 4 * Q, width), BF), vm((C, 2, Q, width), F32), vm((C, 2, 3, Q, width), BF),
            vm((C, Q, width), far_type), vm((C, Q, width), far_type),
        ]

    vspec = pl.BlockSpec(memory_space=pltpu.VMEM)
    anys = pl.BlockSpec(memory_space=pl.ANY)
    return pl.pallas_call(
        kernel,
        out_shape=(
            jax.ShapeDtypeStruct((32, D), BF),
            jax.ShapeDtypeStruct((32, D), BF),
            jax.ShapeDtypeStruct((D, H), F32),
            jax.ShapeDtypeStruct((D, H), F32),
            jax.ShapeDtypeStruct((H, D), F32),
        ),
        in_specs=[vspec] * 5 + [pl.BlockSpec(memory_space=pltpu.SMEM)],
        out_specs=(vspec, vspec, anys, anys, anys),
        scratch_shapes=[
            vm((D, 2 * H), BF), vm((H, D), BF), vm((C, T, D), BF), vm((C, CHIP, H), BF), vm((4 * Q, 2 * H), F32),
            *scatter_tok_scratch(2 * H, F32), vm((C, Q, 2 * H), F32), vm((C, T, H), BF),
            *scatter_hid_scratch(),
            vm((C, T, D), BF), *scatter_tok_scratch(H, BF), vm((C, T, 2 * H), BF),
            *scatter_hid_scratch(),
            vm((D, 2 * H), F32), vm((H, D), F32),
            pltpu.SemaphoreType.DMA((COPIES,)), pltpu.SemaphoreType.DMA((COPIES,)), pltpu.SemaphoreType.DMA((8,)),
        ],
        compiler_params=pltpu.CompilerParams(
            collective_id=0, has_side_effects=True, vmem_limit_bytes=56 << 20
        ),
        cost_estimate=pl.CostEstimate(flops=9663676416, bytes_accessed=10 << 20, transcendentals=262144),
    )(student_in, target_delta, gate_weight, up_weight, down_weight, block_mask)


def solution(mesh):
    placed = (
        P("hid", "tok"),
        P("hid", "tok"),
        P("tok", "hid"),
        P("tok", "hid"),
        P("hid", "tok"),
        P(None, "tok", "hid"),
    )
    return jax.shard_map(
        per_device,
        mesh=mesh,
        in_specs=placed,
        out_specs=(
            P("hid", "tok"),
            P("hid", "tok"),
            P("tok", "hid"),
            P("tok", "hid"),
            P("hid", "tok"),
        ),
        check_vma=False,
    )
```

time: 857 us -> 208 us (0.24)
  waiting for transfers between devices: 783 us -> 0 us
  Pallas kernels: 0 us -> 196 us
  matrix products: 34.4 us -> 0 us
  between operations: 14 us -> 0.64 us
  other arithmetic: 10.7 us -> 0 us
    reduce_scatter x4 -> x0, waiting for transfers between devices: 484 us -> none  [the longest x1 142 us: per_device(): lax.psum_scatter(jnp.dot(piece, down_eff, preferred_element_type=jnp.floa...]
    all_gather x5 -> x0, waiting for transfers between devices: 298 us -> none  [the longest x1 63.9 us: per_device(): inputs_all = lax.all_gather(student_in, 'hid', axis=0, tiled=True)]
    pallas_call x0 -> x1, Pallas kernels: none -> 196 us  [per_device(): pl.pallas_call(kernel, out_shape=(jax.ShapeDtypeStruct((32, D), BF), jax....]
    dot_general x9 -> x0, matrix products: 34.4 us -> none  [the longest x1 5.75 us: per_device(): lax.dot_general(up_grad_all, up_eff, by_cols, preferred_element_type=jnp....]
  transfers between devices with their start and end apart: 9 -> 0, of which waited for: 9 -> 0; matrix products, arithmetic and copies ran while one was open for 3% -> 0% of each run, Pallas kernels for 0% -> 0%
where the time goes in v1:
time: 208 us
  Pallas kernels  196 us (94%)
  local copies, waits for them, and re-layouts  11.2 us (5%)
    pallas_call x1, Pallas kernels, per_device(): pl.pallas_call(kernel, out_shape=(jax.ShapeDtypeStruct((32, D), BF), jax....  196 us
    unnamed x10, local copies, waits for them, and re-layouts  11.2 us

profile of v1, /device:TPU:1, one launch (start us, length us, event | category | flops | bytes accessed | tf_op | source)
XLA Modules:
  0.0 207.9 jit_solution(11388667542813525454)
XLA Ops:
  0.6 1.4 copy.11.bm
  2.0 196.0 %shard_map.101 = (bf16[32,1024]{1,0:T(8,128)(2,1)}, bf16[32,1024]{1,0:T(8,128)(2,1)}, f32[1024,512]{1,0:T(8,128)}, f32[1024,512]{1,0:T(8,128)}, f32[512,1024]{1,0:T(8,128)}) custom-call(bf16[32,1024]{1,0:T(8,128)(2,1)} %x_in.1, bf16[32,1024]{1,0:T(8,128)(2,1)} %t_in.1, bf16[1024,512]{1,0:T(8,128)(2,1)} %gw.1, bf16[1024,512]{1,0:T(8,128)(2,1)} %uw.1, ...), custom_call_target="tpu_custom_call" | custom-call | flops 9663676416 | bytes 10485760 | tf_op jit(solution)/shard_map/pallas_call | solution.py:330
  198.0 1.5 copy.17
  199.5 1.5 copy.18
  201.0 0.0 copy-start.1
  201.0 3.2 %copy.19 = f32[1024,512]{1,0:T(8,128)} copy(f32[1024,512]{1,0:T(8,128)} %get-tuple-element.12) | data formatting | bytes 4194304
  204.2 0.0 copy-done.1
  204.2 0.0 copy-start
  204.2 1.3 copy.20
  205.5 1.0 copy-done
  206.6 1.3 copy.21
Async XLA Ops:
  201.0 3.2 %copy-start.1 = (f32[1024,512]{1,0:T(8,128)S(1)}, f32[1024,512]{1,0:T(8,128)}, u32[]{:S(2)}) copy-start(f32[1024,512]{1,0:T(8,128)} %get-tuple-element.13) | copy-start | bytes 6291460
  204.2 2.3 %copy-start = (f32[512,1024]{1,0:T(8,128)S(1)}, f32[512,1024]{1,0:T(8,128)}, u32[]{:S(2)}) copy-start(f32[512,1024]{1,0:T(8,128)} %get-tuple-element.14) | copy-start | bytes 6291460

commit v2 on v1

v2 whole, which is shorter than its diff:
```python
import jax
import jax.numpy as jnp
from jax import lax
from jax.experimental import pallas as pl
from jax.experimental.pallas import tpu as pltpu
from jax.sharding import PartitionSpec as P

BF = jnp.bfloat16
F32 = jnp.float32
CHUNKS = 4
T = 256
CHIP = 16
XB = 4 * CHIP
Q = 32
D = 1024
H = 512
COPIES = 256
STEPS = 23
LAG = 1

NN = (((1,), (0,)), ((), ()))
NT = (((1,), (1,)), ((), ()))
TN = (((0,), (0,)), ((), ()))


def mm(a, b, dims):
    return lax.dot_general(a, b, dims, preferred_element_type=F32)


def kernel(
    x_in, t_in, gw, uw, dw, bm,
    out, ig, x_out, h_out, e_out, g_out,
    weff, deff, xall, tch, tmp, ps2, own2, yl2, zs2, zl2, gu, hall,
    ss4, sl4, of4, xs4, xl4, zs4, zl4, osw, oland,
    eall, ps6, own6, yl6, zs6, zl6, gall,
    ss8, sl8, of8, xs8, xl8, zs8, zl8, isw, iland,
    send_sems, recv_sems, loc_sems,
):
    tok = lax.axis_index("tok")
    hid = lax.axis_index("hid")
    y, zh = lax.div(tok, 2), lax.rem(tok, 2)
    c, x, zl = lax.rem(hid, 2), lax.rem(lax.div(hid, 2), 4), lax.div(hid, 8)

    def dev(y=y, zh=zh, zl=zl, x=x, c=c):
        return {"tok": y * 2 + zh, "hid": (zl * 4 + x) * 2 + c}

    def plus(a, d):
        return lax.rem(a + d, 4)

    sib = dev(c=1 - c)
    xp = [dev(x=plus(x, d)) for d in (1, 2, 3)]
    zp = [dev(zl=plus(zl, d)) for d in (1, 2, 3)]
    yp = [dev(y=plus(y, d)) for d in (1, 2, 3)]
    far = dev(zh=1 - zh)
    peers = [sib, far] + xp + zp + yp

    def rows(start, size):
        return pl.ds(pl.multiple_of(start, 16), size)

    def half(which):
        return pl.ds(pl.multiple_of(which * H, H), H)

    mine, other = half(c), half(1 - c)
    copies = []

    def send(src, dst, device):
        i = len(copies)
        copy = pltpu.make_async_remote_copy(
            src_ref=src, dst_ref=dst, send_sem=send_sems.at[i], recv_sem=recv_sems.at[i],
            device_id=device, device_id_type=pl.DeviceIdType.MESH,
        )
        copy.start()
        copies.append(copy)
        return copy

    def arrived(group):
        for copy in group:
            copy.wait_recv()

    locals_ = []

    def local(src, dst):
        copy = pltpu.make_async_copy(src, dst, loc_sems.at[len(locals_)])
        copy.start()
        locals_.append(copy)
        return copy

    barrier = pltpu.get_barrier_semaphore()
    for peer in peers:
        pl.semaphore_signal(barrier, inc=1, device_id=peer, device_id_type=pl.DeviceIdType.MESH)
    pl.semaphore_wait(barrier, len(peers))

    block = x * XB + zl * CHIP
    first = []
    for whole, buf, at in ((x_in, xall, block), (t_in, tch, 0)):
        for j in range(2):
            src = whole.at[pl.ds(j * CHIP, CHIP)]
            dst = buf.at[2 * c + j, rows(at, CHIP)]
            if whole is x_in:
                first.append([send(src.at[:, other], dst.at[:, other], sib), local(src.at[:, mine], dst.at[:, mine])])
            else:
                first.append([send(src.at[:, other], dst, sib), local(src.at[:, mine], dst)])

    def mask_weights():
        @pl.loop(0, 8)
        def _(a):
            at = pl.ds(pl.multiple_of(a * 128, 128), 128)
            for b in range(4):
                lanes = pl.ds(b * 128, 128)
                weff[at, lanes] = (gw[at, lanes].astype(F32) * bm[0, a, b].astype(F32)).astype(BF)
                weff[at, pl.ds(H + b * 128, 128)] = (
                    uw[at, lanes].astype(F32) * bm[1, a, b].astype(F32)
                ).astype(BF)
                deff[lanes, at] = (dw[lanes, at].astype(F32) * bm[2, a, b].astype(F32)).astype(BF)

    def gather_hid(k, buf):
        own = buf.at[k, rows(block, CHIP), mine]
        zc = [send(own, own, p) for p in zp]
        yield
        arrived(zc)
        col = buf.at[k, rows(x * XB, XB), mine]
        xc = [send(col, col, p) for p in xp]
        sc = [send(col, col, sib)]
        yield
        for d, xcopy in enumerate(xc):
            arrived([xcopy])
            got = buf.at[k, rows(plus(x, 3 - d) * XB, XB), mine]
            sc.append(send(got, got, sib))
        yield
        arrived(sc)

    def scatter_tok(k, product, ps, own, yland, zs, zland, width):
        @pl.loop(0, width // H)
        def _(n):
            lanes = pl.ds(pl.multiple_of(n * H, H), H)
            value = product(k, lanes)
            tmp[:, lanes] = value
            ps[k, :, lanes] = value.astype(BF)

        yc = []
        for part in range(2):
            base = (1 - zh if part == 0 else zh) * 4 * Q
            own[k, part] = tmp[rows(base + y * Q, Q), pl.ds(0, width)]
            yc.append([send(ps.at[k, rows(base + plus(y, d) * Q, Q)], yland.at[k, part, 3 - d], yp[d - 1])
                       for d in (2, 1, 3)])
        yield
        arrived(yc[0])
        total = own[k, 0]
        for d in range(3):
            total = total + yland[k, 0, d].astype(F32)
        zs[k] = total.astype(zs.dtype)
        zc = send(zs.at[k], zland.at[k], far)
        yield
        arrived(yc[1])
        total = own[k, 1]
        for d in range(3):
            total = total + yland[k, 1, d].astype(F32)
        own[k, 1] = total
        yield
        arrived([zc])

    def gather_tok(k, buf):
        own = buf.at[k, rows(zh * 4 * Q + y * Q, Q)]
        zc = send(own, own, far)
        yc = [send(own, own, p) for p in yp]
        yield
        arrived([zc])
        got = buf.at[k, rows((1 - zh) * 4 * Q + y * Q, Q)]
        yc += [send(got, got, p) for p in yp]
        yield
        arrived(yc)

    def scatter_hid(k, product, ss, sl, of, xs, xl, zs, zland):
        ss[k] = product(k, other).astype(ss.dtype)
        sc = send(ss.at[k], sl.at[k], sib)
        of[k] = product(k, mine)
        yield
        arrived([sc])
        xc = []
        for d in (2, 1, 3):
            at = rows(plus(x, d) * XB, XB)
            xs[k, d - 1] = (of[k, at] + sl[k, at].astype(F32)).astype(BF)
            xc.append(send(xs.at[k, d - 1], xl.at[k, 3 - d], xp[d - 1]))
        at = rows(x * XB, XB)
        of[k, at] = of[k, at] + sl[k, at].astype(F32)
        yield
        arrived(xc)
        total = of[k, at]
        for d in range(3):
            total = total + xl[k, d].astype(F32)
        of[k, at] = total
        zc = []
        for d in (1, 2, 3):
            zs[k, d - 1] = of[k, rows(x * XB + plus(zl, d) * CHIP, CHIP)].astype(BF)
            zc.append(send(zs.at[k, d - 1], zland.at[k, 3 - d], zp[d - 1]))
        yield
        arrived(zc)

    def scattered(k, of, zland):
        total = of[k, rows(block, CHIP)]
        for d in range(3):
            total = total + zland[k, d].astype(F32)
        return total

    def chain(k):
        panel = rows(zh * 4 * Q + y * Q, Q)
        tokens = pl.ds(k * T, T)
        yield from gather_hid(k, xall)
        local(xall.at[k], x_out.at[tokens])

        def inputs_by_weights(k, lanes):
            return mm(xall[k], weff[:, lanes], NN)

        yield from scatter_tok(k, inputs_by_weights, ps2, own2, yl2, zs2, zl2, 2 * H)
        gu[k] = own2[k, 1] + zl2[k].astype(F32)
        gate, up = gu[k, :, :H], gu[k, :, H:]
        hall[k, panel, :] = (gate * jax.nn.sigmoid(gate) * up).astype(BF)
        yield from gather_tok(k, hall)
        local(hall.at[k], h_out.at[tokens])

        def hidden_by_down(k, lanes):
            return mm(hall[k], deff[:, lanes], NN)

        yield from scatter_hid(k, hidden_by_down, ss4, sl4, of4, xs4, xl4, zs4, zl4)
        total = scattered(k, of4, zl4)
        eall[k, rows(block, CHIP), mine] = (total - tch[k].astype(F32)).astype(BF)
        osw[k] = total.astype(BF)
        yield from gather_hid(k, eall)
        local(eall.at[k], e_out.at[tokens])

        def error_by_down(k, lanes):
            return mm(eall[k], deff[...], NT)

        yield from scatter_tok(k, error_by_down, ps6, own6, yl6, zs6, zl6, H)
        hidden_grad = own6[k, 1] + zl6[k].astype(F32)
        gate, up = gu[k, :, :H], gu[k, :, H:]
        sigma = jax.nn.sigmoid(gate)
        gall[k, panel, :H] = (hidden_grad * up * (sigma + gate * sigma * (1.0 - sigma))).astype(BF)
        gall[k, panel, H:] = (hidden_grad * (gate * sigma)).astype(BF)
        yield from gather_tok(k, gall)
        local(gall.at[k], g_out.at[tokens])

        def grads_by_weights(k, which):
            return mm(gall[k], weff[which, :], NT)

        yield from scatter_hid(k, grads_by_weights, ss8, sl8, of8, xs8, xl8, zs8, zl8)
        isw[k] = scattered(k, of8, zl8).astype(BF)

    for remote, near in first:
        arrived([remote])
        near.wait()
    chains = [chain(k) for k in range(CHUNKS)]
    for step in range(STEPS + LAG * (CHUNKS - 1)):
        for k in range(CHUNKS):
            if 0 <= step - k * LAG < STEPS:
                next(chains[k], None)
        if step == 0:
            mask_weights()
    swaps = [[send(held.at[2 * (1 - c) + j], land.at[j], sib) for j in range(2)]
             for held, land in ((osw, oland), (isw, iland))]
    for j in range(2):
        at = pl.ds(j * CHIP, CHIP)
        for swap, held, land, result in zip(swaps, (osw, isw), (oland, iland), (out, ig)):
            result[at, mine] = held[2 * c + j]
            arrived([swap[j]])
            result[at, other] = land[j]
    for copy in copies:
        copy.wait_send()
    for copy in locals_[4:]:
        copy.wait()


def weight_grads(bm, x, h, e, g, out_in, ig_in, out, ig, gwg, uwg, dwg):
    p = pl.program_id(0)
    out[...] = out_in[...]
    ig[...] = ig_in[...]
    value = mm(x[...], g[...], TN)
    for i in range(2):
        for b in range(8):
            to = (gwg, uwg)[b // 4]
            to[pl.ds(i * 128, 128), pl.ds(b % 4 * 128, 128)] = (
                value[i * 128 : i * 128 + 128, b * 128 : b * 128 + 128]
                * (bm[b // 4, p * 2 + i, b % 4].astype(F32) * (1.0 / 32.0))
            )
    value = mm(h[...], e[...], TN)
    for a in range(8):
        dwg[:, pl.ds(a * 128, 128)] = value[:, a * 128 : a * 128 + 128] * (
            bm[2, a, p].astype(F32) * (1.0 / 32.0)
        )


def per_device(student_in, target_delta, gate_weight, up_weight, down_weight, block_mask):
    C = CHUNKS
    vm = pltpu.VMEM

    def scatter_hid_scratch():
        return [
            vm((C, T, H), F32), vm((C, T, H), F32), vm((C, T, H), F32), vm((C, 3, XB, H), BF), vm((C, 3, XB, H), BF),
            vm((C, 3, CHIP, H), BF), vm((C, 3, CHIP, H), BF), vm((C, CHIP, H), BF), vm((2, CHIP, H), BF),
        ]

    def scatter_tok_scratch(width, far_type):
        return [
            vm((C, T, width), BF), vm((C, 2, Q, width), F32), vm((C, 2, 3, Q, width), BF),
            vm((C, Q, width), far_type), vm((C, Q, width), far_type),
        ]

    vspec = pl.BlockSpec(memory_space=pltpu.VMEM)
    anys = pl.BlockSpec(memory_space=pl.ANY)
    small, square = jax.ShapeDtypeStruct((2 * CHIP, D), BF), jax.ShapeDtypeStruct((C * T, D), BF)
    out, ig, x, h, e, g = pl.pallas_call(
        kernel,
        out_shape=(small, small, square, jax.ShapeDtypeStruct((C * T, H), BF), square, square),
        in_specs=[vspec] * 5 + [pl.BlockSpec(memory_space=pltpu.SMEM)],
        out_specs=(vspec, vspec, anys, anys, anys, anys),
        scratch_shapes=[
            vm((D, 2 * H), BF), vm((H, D), BF), vm((C, T, D), BF), vm((C, CHIP, H), BF), vm((T, 2 * H), F32),
            *scatter_tok_scratch(2 * H, F32), vm((C, Q, 2 * H), F32), vm((C, T, H), BF),
            *scatter_hid_scratch(),
            vm((C, T, D), BF), *scatter_tok_scratch(H, BF), vm((C, T, 2 * H), BF),
            *scatter_hid_scratch(),
            pltpu.SemaphoreType.DMA((COPIES,)), pltpu.SemaphoreType.DMA((COPIES,)), pltpu.SemaphoreType.DMA((20,)),
        ],
        compiler_params=pltpu.CompilerParams(
            collective_id=0, has_side_effects=True, vmem_limit_bytes=56 << 20
        ),
        cost_estimate=pl.CostEstimate(flops=6442450944, bytes_accessed=10 << 20, transcendentals=262144),
    )(student_in, target_delta, gate_weight, up_weight, down_weight, block_mask)
    full = lambda *shape: pl.BlockSpec(shape, lambda p: (0, 0))
    return pl.pallas_call(
        weight_grads,
        grid=(4,),
        out_shape=(
            small,
            small,
            jax.ShapeDtypeStruct((D, H), F32),
            jax.ShapeDtypeStruct((D, H), F32),
            jax.ShapeDtypeStruct((H, D), F32),
        ),
        in_specs=[
            pl.BlockSpec(memory_space=pltpu.SMEM),
            pl.BlockSpec((C * T, 256), lambda p: (0, p)),
            pl.BlockSpec((C * T, 128), lambda p: (0, p)),
            full(C * T, D),
            full(C * T, D),
            full(2 * CHIP, D),
            full(2 * CHIP, D),
        ],
        out_specs=(
            full(2 * CHIP, D),
            full(2 * CHIP, D),
            pl.BlockSpec((256, H), lambda p: (p, 0)),
            pl.BlockSpec((256, H), lambda p: (p, 0)),
            pl.BlockSpec((128, D), lambda p: (p, 0)),
        ),
        compiler_params=pltpu.CompilerParams(vmem_limit_bytes=40 << 20),
        cost_estimate=pl.CostEstimate(flops=3221225472, bytes_accessed=13 << 20, transcendentals=0),
    )(block_mask, x, h, e, g, out, ig)


def solution(mesh):
    placed = (
        P("hid", "tok"),
        P("hid", "tok"),
        P("tok", "hid"),
        P("tok", "hid"),
        P("hid", "tok"),
        P(None, "tok", "hid"),
    )
    return jax.shard_map(
        per_device,
        mesh=mesh,
        in_specs=placed,
        out_specs=(
            P("hid", "tok"),
            P("hid", "tok"),
            P("tok", "hid"),
            P("tok", "hid"),
            P("hid", "tok"),
        ),
        check_vma=False,
    )
```

time: 208 us -> 155 us (0.75)
  Pallas kernels: 196 us -> 145 us
  local copies, waits for them, and re-layouts: 11.2 us -> 9.05 us
    pallas_call x1 -> x2, Pallas kernels: 196 us -> 145 us  [the longest x1 139 us: per_device(): pl.pallas_call(kernel, out_shape=(small, small, square, jax.ShapeDtypeStr...]
    unnamed x10 -> x15, local copies, waits for them, and re-layouts: 11.2 us -> 9.05 us
where the time goes in v2:
time: 155 us
  Pallas kernels  145 us (94%)
  local copies, waits for them, and re-layouts  9.05 us (6%)
    pallas_call x1, Pallas kernels, per_device(): pl.pallas_call(kernel, out_shape=(small, small, square, jax.ShapeDtypeStr...  139 us
    unnamed x15, local copies, waits for them, and re-layouts  9.05 us
    pallas_call x1, Pallas kernels, per_device(): pl.pallas_call(weight_grads, grid=(4,), out_shape=(small, small, jax.Shap...  6.21 us

profile of v2, /device:TPU:1, one launch (start us, length us, event | category | flops | bytes accessed | tf_op | source)
XLA Modules:
  0.0 154.9 jit_solution(445007018312058354)
XLA Ops:
  0.6 1.4 copy.12.bm
  2.0 0.0 copy-start
  2.0 138.9 %shard_map.101 = (bf16[32,1024]{1,0:T(8,128)(2,1)}, bf16[32,1024]{1,0:T(8,128)(2,1)}, bf16[1024,1024]{1,0:T(8,128)(2,1)}, bf16[1024,512]{1,0:T(8,128)(2,1)}, bf1...) custom-call(bf16[32,1024]{1,0:T(8,128)(2,1)} %x_in.1, bf16[32,1024]{1,0:T(8,128)(2,1)} %t_in.1, bf16[1024,512]{1,0:T(8,128)(2,1)} %gw.1, ...), custom_call_target="tpu_custom_call" | custom-call | flops 6442450944 | bytes 10485760 | tf_op jit(solution)/shard_map/pallas_call | solution.py:311
  140.9 0.0 copy-done
  141.0 0.0 copy-start.1
  141.0 1.6 %copy-done.1 = bf16[1024,1024]{1,0:T(8,128)(2,1)S(1)} copy-done((bf16[1024,1024]{1,0:T(8,128)(2,1)S(1)}, bf16[1024,1024]{1,0:T(8,128)(2,1)}, u32[]{:S(2)}) %copy-start.1) | copy-done | bytes 2097176
  142.6 0.0 copy-start.2
  142.6 1.6 %copy-done.2 = bf16[1024,1024]{1,0:T(8,128)(2,1)S(1)} copy-done((bf16[1024,1024]{1,0:T(8,128)(2,1)S(1)}, bf16[1024,1024]{1,0:T(8,128)(2,1)}, u32[]{:S(2)}) %copy-start.2) | copy-done | bytes 2097176
  144.1 0.0 copy-start.3
  144.1 1.6 %copy-done.3 = bf16[1024,1024]{1,0:T(8,128)(2,1)S(1)} copy-done((bf16[1024,1024]{1,0:T(8,128)(2,1)S(1)}, bf16[1024,1024]{1,0:T(8,128)(2,1)}, u32[]{:S(2)}) %copy-start.3) | copy-done | bytes 2097176
  145.7 0.0 copy-start.4
  145.7 1.2 copy-done.4
  147.0 0.0 copy-start.5
  147.0 0.8 copy-done.5
  147.8 0.0 copy-start.6
  147.8 0.8 copy-done.6
  148.6 6.2 %shard_map.102 = (bf16[32,1024]{1,0:T(8,128)(2,1)}, bf16[32,1024]{1,0:T(8,128)(2,1)}, f32[1024,512]{1,0:T(8,128)}, f32[1024,512]{1,0:T(8,128)}, f32[512,1024]{1,0:T(8,128)}) custom-call(s32[3,8,4]{2,1,0:T(8,128)S(1)} %copy-done, bf16[1024,1024]{1,0:T(8,128)(2,1)S(1)} %copy-done.1, bf16[1024,512]{1,0:T(8,128)(2,1)S(1)} %copy-done.4, ...), custom_call_target="tpu_custom_call" | custom-call | flops 3221225472 | bytes 13631488 | tf_op jit(solution)/shard_map/pallas_call | solution.py:330
Async XLA Ops:
  2.0 138.9 %copy-start = (s32[3,8,4]{2,1,0:T(8,128)S(1)}, s32[3,8,4]{2,1,0:T(8,128)}, u32[]{:S(2)}) copy-start(s32[3,8,4]{2,1,0:T(8,128)} %copy.12.bm) | copy-start | bytes 1156
  141.0 1.6 %copy-start.1 = (bf16[1024,1024]{1,0:T(8,128)(2,1)S(1)}, bf16[1024,1024]{1,0:T(8,128)(2,1)}, u32[]{:S(2)}) copy-start(bf16[1024,1024]{1,0:T(8,128)(2,1)} %get-tuple-element.11.x) | copy-start | bytes 6291460
  142.6 1.6 %copy-start.2 = (bf16[1024,1024]{1,0:T(8,128)(2,1)S(1)}, bf16[1024,1024]{1,0:T(8,128)(2,1)}, u32[]{:S(2)}) copy-start(bf16[1024,1024]{1,0:T(8,128)(2,1)} %get-tuple-element.13.e) | copy-start | bytes 6291460
  144.1 1.6 %copy-start.3 = (bf16[1024,1024]{1,0:T(8,128)(2,1)S(1)}, bf16[1024,1024]{1,0:T(8,128)(2,1)}, u32[]{:S(2)}) copy-start(bf16[1024,1024]{1,0:T(8,128)(2,1)} %get-tuple-element.14.g) | copy-start | bytes 6291460
  145.7 1.2 copy-start.4
  147.0 0.8 copy-start.5
  147.8 0.8 copy-start.6

commit v3 on v2

--- a/solution.py
+++ b/solution.py
@@ -14,7 +14,7 @@
 Q = 32
 D = 1024
 H = 512
-COPIES = 256
+COPIES = 112
 STEPS = 23
 LAG = 1
 
@@ -28,12 +28,13 @@
 
 
 def kernel(
-    x_in, t_in, gw, uw, dw, bm,
+    x_in, t_in, gw_in, uw_in, dw_in, bm_in,
     out, ig, x_out, h_out, e_out, g_out,
     weff, deff, xall, tch, tmp, ps2, own2, yl2, zs2, zl2, gu, hall,
     ss4, sl4, of4, xs4, xl4, zs4, zl4, osw, oland,
     eall, ps6, own6, yl6, zs6, zl6, gall,
     ss8, sl8, of8, xs8, xl8, zs8, zl8, isw, iland,
+    gw, uw, dw, bm,
     send_sems, recv_sems, loc_sems,
 ):
     tok = lax.axis_index("tok")
@@ -61,21 +62,22 @@
         return pl.ds(pl.multiple_of(which * H, H), H)
 
     mine, other = half(c), half(1 - c)
-    copies = []
-
-    def send(src, dst, device):
-        i = len(copies)
-        copy = pltpu.make_async_remote_copy(
-            src_ref=src, dst_ref=dst, send_sem=send_sems.at[i], recv_sem=recv_sems.at[i],
-            device_id=device, device_id_type=pl.DeviceIdType.MESH,
+    groups = []
+
+    def send(pairs, whole):
+        i = len(groups)
+        for src, dst, device in pairs:
+            pltpu.make_async_remote_copy(
+                src_ref=src, dst_ref=dst, send_sem=send_sems.at[i], recv_sem=recv_sems.at[i],
+                device_id=device, device_id_type=pl.DeviceIdType.MESH,
+            ).start()
+        groups.append(
+            pltpu.make_async_remote_copy(
+                src_ref=whole, dst_ref=whole, send_sem=send_sems.at[i], recv_sem=recv_sems.at[i],
+                device_id=sib, device_id_type=pl.DeviceIdType.MESH,
+            )
         )
-        copy.start()
-        copies.append(copy)
-        return copy
-
-    def arrived(group):
-        for copy in group:
-            copy.wait_recv()
+        return groups[-1]
 
     locals_ = []
 
@@ -88,6 +90,8 @@
     barrier = pltpu.get_barrier_semaphore()
     for peer in peers:
         pl.semaphore_signal(barrier, inc=1, device_id=peer, device_id_type=pl.DeviceIdType.MESH)
+    for whole, held in ((bm_in, bm), (gw_in, gw), (uw_in, uw), (dw_in, dw)):
+        local(whole, held)
     pl.semaphore_wait(barrier, len(peers))
 
     block = x * XB + zl * CHIP
@@ -97,37 +101,42 @@
             src = whole.at[pl.ds(j * CHIP, CHIP)]
             dst = buf.at[2 * c + j, rows(at, CHIP)]
             if whole is x_in:
-                first.append([send(src.at[:, other], dst.at[:, other], sib), local(src.at[:, mine], dst.at[:, mine])])
+                first.append(send([(src.at[:, other], dst.at[:, other], sib)], dst.at[:, other]))
+                local(src.at[:, mine], dst.at[:, mine])
             else:
-                first.append([send(src.at[:, other], dst, sib), local(src.at[:, mine], dst)])
+                first.append(send([(src.at[:, other], dst, sib)], dst))
+                local(src.at[:, mine], dst)
 
     def mask_weights():
+        for copy in locals_[:4]:
+            copy.wait()
+
         @pl.loop(0, 8)
         def _(a):
             at = pl.ds(pl.multiple_of(a * 128, 128), 128)
             for b in range(4):
                 lanes = pl.ds(b * 128, 128)
-                weff[at, lanes] = (gw[at, lanes].astype(F32) * bm[0, a, b].astype(F32)).astype(BF)
+                weff[at, lanes] = (gw[at, lanes].astype(F32) * bm[0, b, a].astype(F32)).astype(BF)
                 weff[at, pl.ds(H + b * 128, 128)] = (
-                    uw[at, lanes].astype(F32) * bm[1, a, b].astype(F32)
+                    uw[at, lanes].astype(F32) * bm[1, b, a].astype(F32)
                 ).astype(BF)
-                deff[lanes, at] = (dw[lanes, at].astype(F32) * bm[2, a, b].astype(F32)).astype(BF)
+                deff[lanes, at] = (dw[lanes, at].astype(F32) * bm[2, b, a].astype(F32)).astype(BF)
 
     def gather_hid(k, buf):
         own = buf.at[k, rows(block, CHIP), mine]
-        zc = [send(own, own, p) for p in zp]
-        yield
-        arrived(zc)
+        zc = send([(own, own, p) for p in zp], buf.at[k, pl.ds(0, 3 * CHIP), mine])
+        yield
+        zc.wait_recv()
         col = buf.at[k, rows(x * XB, XB), mine]
-        xc = [send(col, col, p) for p in xp]
-        sc = [send(col, col, sib)]
-        yield
-        for d, xcopy in enumerate(xc):
-            arrived([xcopy])
-            got = buf.at[k, rows(plus(x, 3 - d) * XB, XB), mine]
-            sc.append(send(got, got, sib))
-        yield
-        arrived(sc)
+        xc = send([(col, col, xp[d - 1]) for d in (2, 1, 3)], buf.at[k, pl.ds(0, 3 * XB), mine])
+        s1 = send([(col, col, sib)], col)
+        yield
+        xc.wait_recv()
+        got = [buf.at[k, rows(plus(x, d) * XB, XB), mine] for d in (1, 2, 3)]
+        s2 = send([(g, g, sib) for g in got], buf.at[k, pl.ds(0, 3 * XB), mine])
+        yield
+        s1.wait_recv()
+        s2.wait_recv()
 
     def scatter_tok(k, product, ps, own, yland, zs, zland, width):
         @pl.loop(0, width // H)
@@ -141,60 +150,64 @@
         for part in range(2):
             base = (1 - zh if part == 0 else zh) * 4 * Q
             own[k, part] = tmp[rows(base + y * Q, Q), pl.ds(0, width)]
-            yc.append([send(ps.at[k, rows(base + plus(y, d) * Q, Q)], yland.at[k, part, 3 - d], yp[d - 1])
-                       for d in (2, 1, 3)])
-        yield
-        arrived(yc[0])
+            yc.append(send([(ps.at[k, rows(base + plus(y, d) * Q, Q)], yland.at[k, part, 3 - d], yp[d - 1])
+                            for d in (2, 1, 3)], yland.at[k, part]))
+        yield
+        yc[0].wait_recv()
         total = own[k, 0]
         for d in range(3):
             total = total + yland[k, 0, d].astype(F32)
         zs[k] = total.astype(zs.dtype)
-        zc = send(zs.at[k], zland.at[k], far)
-        yield
-        arrived(yc[1])
+        zc = send([(zs.at[k], zland.at[k], far)], zland.at[k])
+        yield
+        yc[1].wait_recv()
         total = own[k, 1]
         for d in range(3):
             total = total + yland[k, 1, d].astype(F32)
         own[k, 1] = total
         yield
-        arrived([zc])
+        zc.wait_recv()
 
     def gather_tok(k, buf):
         own = buf.at[k, rows(zh * 4 * Q + y * Q, Q)]
-        zc = send(own, own, far)
-        yc = [send(own, own, p) for p in yp]
-        yield
-        arrived([zc])
+        three = buf.at[k, pl.ds(0, 3 * Q)]
+        zc = send([(own, own, far)], own)
+        y1 = send([(own, own, yp[d - 1]) for d in (2, 1, 3)], three)
+        yield
+        zc.wait_recv()
         got = buf.at[k, rows((1 - zh) * 4 * Q + y * Q, Q)]
-        yc += [send(got, got, p) for p in yp]
-        yield
-        arrived(yc)
+        y2 = send([(got, got, yp[d - 1]) for d in (2, 1, 3)], three)
+        yield
+        y1.wait_recv()
+        y2.wait_recv()
 
     def scatter_hid(k, product, ss, sl, of, xs, xl, zs, zland):
         ss[k] = product(k, other).astype(ss.dtype)
-        sc = send(ss.at[k], sl.at[k], sib)
+        sc = send([(ss.at[k], sl.at[k], sib)], sl.at[k])
         of[k] = product(k, mine)
         yield
-        arrived([sc])
-        xc = []
+        sc.wait_recv()
+        pairs = []
         for d in (2, 1, 3):
             at = rows(plus(x, d) * XB, XB)
             xs[k, d - 1] = (of[k, at] + sl[k, at].astype(F32)).astype(BF)
-            xc.append(send(xs.at[k, d - 1], xl.at[k, 3 - d], xp[d - 1]))
+            pairs.append((xs.at[k, d - 1], xl.at[k, 3 - d], xp[d - 1]))
+        xc = send(pairs, xl.at[k])
         at = rows(x * XB, XB)
         of[k, at] = of[k, at] + sl[k, at].astype(F32)
         yield
-        arrived(xc)
+        xc.wait_recv()
         total = of[k, at]
         for d in range(3):
             total = total + xl[k, d].astype(F32)
         of[k, at] = total
-        zc = []
+        pairs = []
         for d in (1, 2, 3):
             zs[k, d - 1] = of[k, rows(x * XB + plus(zl, d) * CHIP, CHIP)].astype(BF)
-            zc.append(send(zs.at[k, d - 1], zland.at[k, 3 - d], zp[d - 1]))
-        yield
-        arrived(zc)
+            pairs.append((zs.at[k, d - 1], zland.at[k, 3 - d], zp[d - 1]))
+        zc = send(pairs, zland.at[k])
+        yield
+        zc.wait_recv()
 
     def scattered(k, of, zland):
         total = of[k, rows(block, CHIP)]
@@ -246,9 +259,10 @@
         yield from scatter_hid(k, grads_by_weights, ss8, sl8, of8, xs8, xl8, zs8, zl8)
         isw[k] = scattered(k, of8, zl8).astype(BF)
 
-    for remote, near in first:
-        arrived([remote])
-        near.wait()
+    for group in first:
+        group.wait_recv()
+    for copy in locals_[4:]:
+        copy.wait()
     chains = [chain(k) for k in range(CHUNKS)]
     for step in range(STEPS + LAG * (CHUNKS - 1)):
         for k in range(CHUNKS):
@@ -256,17 +270,17 @@
                 next(chains[k], None)
         if step == 0:
             mask_weights()
-    swaps = [[send(held.at[2 * (1 - c) + j], land.at[j], sib) for j in range(2)]
+    swaps = [send([(held.at[2 * (1 - c) + j], land.at[j], sib) for j in range(2)], land)
              for held, land in ((osw, oland), (isw, iland))]
-    for j in range(2):
-        at = pl.ds(j * CHIP, CHIP)
-        for swap, held, land, result in zip(swaps, (osw, isw), (oland, iland), (out, ig)):
-            result[at, mine] = held[2 * c + j]
-            arrived([swap[j]])
-            result[at, other] = land[j]
-    for copy in copies:
-        copy.wait_send()
-    for copy in locals_[4:]:
+    for swap, held, land, result in zip(swaps, (osw, isw), (oland, iland), (out, ig)):
+        for j in range(2):
+            result[pl.ds(j * CHIP, CHIP), mine] = held[2 * c + j]
+        swap.wait_recv()
+        for j in range(2):
+            result[pl.ds(j * CHIP, CHIP), other] = land[j]
+    for group in groups:
+        group.wait_send()
+    for copy in locals_[8:]:
         copy.wait()
 
 
@@ -280,17 +294,18 @@
             to = (gwg, uwg)[b // 4]
             to[pl.ds(i * 128, 128), pl.ds(b % 4 * 128, 128)] = (
                 value[i * 128 : i * 128 + 128, b * 128 : b * 128 + 128]
-                * (bm[b // 4, p * 2 + i, b % 4].astype(F32) * (1.0 / 32.0))
+                * (bm[b // 4, b % 4, p * 2 + i].astype(F32) * (1.0 / 32.0))
             )
     value = mm(h[...], e[...], TN)
     for a in range(8):
         dwg[:, pl.ds(a * 128, 128)] = value[:, a * 128 : a * 128 + 128] * (
-            bm[2, a, p].astype(F32) * (1.0 / 32.0)
+            bm[2, p, a].astype(F32) * (1.0 / 32.0)
         )
 
 
 def per_device(student_in, target_delta, gate_weight, up_weight, down_weight, block_mask):
     C = CHUNKS
+    block_mask = jnp.swapaxes(block_mask, 1, 2)
     vm = pltpu.VMEM
 
     def scatter_hid_scratch():
@@ -311,7 +326,7 @@
     out, ig, x, h, e, g = pl.pallas_call(
         kernel,
         out_shape=(small, small, square, jax.ShapeDtypeStruct((C * T, H), BF), square, square),
-        in_specs=[vspec] * 5 + [pl.BlockSpec(memory_space=pltpu.SMEM)],
+        in_specs=[pl.BlockSpec(memory_space=pltpu.HBM)] * 6,
         out_specs=(vspec, vspec, anys, anys, anys, anys),
         scratch_shapes=[
             vm((D, 2 * H), BF), vm((H, D), BF), vm((C, T, D), BF), vm((C, CHIP, H), BF), vm((T, 2 * H), F32),
@@ -319,10 +334,11 @@
             *scatter_hid_scratch(),
             vm((C, T, D), BF), *scatter_tok_scratch(H, BF), vm((C, T, 2 * H), BF),
             *scatter_hid_scratch(),
-            pltpu.SemaphoreType.DMA((COPIES,)), pltpu.SemaphoreType.DMA((COPIES,)), pltpu.SemaphoreType.DMA((20,)),
+            vm((D, H), BF), vm((D, H), BF), vm((H, D), BF), pltpu.SMEM((3, 4, 8), jnp.int32),
+            pltpu.SemaphoreType.DMA((COPIES,)), pltpu.SemaphoreType.DMA((COPIES,)), pltpu.SemaphoreType.DMA((24,)),
         ],
         compiler_params=pltpu.CompilerParams(
-            collective_id=0, has_side_effects=True, vmem_limit_bytes=56 << 20
+            collective_id=0, has_side_effects=True, vmem_limit_bytes=62 << 20
         ),
         cost_estimate=pl.CostEstimate(flops=6442450944, bytes_accessed=10 << 20, transcendentals=262144),
     )(student_in, target_delta, gate_weight, up_weight, down_weight, block_mask)
@@ -353,7 +369,7 @@
             pl.BlockSpec((256, H), lambda p: (p, 0)),
             pl.BlockSpec((128, D), lambda p: (p, 0)),
         ),
-        compiler_params=pltpu.CompilerParams(vmem_limit_bytes=40 << 20),
+        compiler_params=pltpu.CompilerParams(vmem_limit_bytes=62 << 20),
         cost_estimate=pl.CostEstimate(flops=3221225472, bytes_accessed=13 << 20, transcendentals=0),
     )(block_mask, x, h, e, g, out, ig)
 

time: 155 us -> 143 us (0.923)
  local copies, waits for them, and re-layouts: 9.05 us -> 0 us
  Pallas kernels: 145 us -> 142 us
    unnamed x15 -> x0, local copies, waits for them, and re-layouts: 9.05 us -> none
    pallas_call x1, Pallas kernels: 139 us -> 134 us  [per_device(): pl.pallas_call(kernel, out_shape=(small, small, square, jax.ShapeDtypeStr...]
    pallas_call x1, Pallas kernels: 6.21 us -> 8.03 us  [per_device(): pl.pallas_call(weight_grads, grid=(4,), out_shape=(small, small, jax.Shap...]
where the time goes in v3:
time: 143 us
  Pallas kernels  142 us (99%)
    pallas_call x1, Pallas kernels, per_device(): pl.pallas_call(kernel, out_shape=(small, small, square, jax.ShapeDtypeStr...  134 us
    pallas_call x1, Pallas kernels, per_device(): pl.pallas_call(weight_grads, grid=(4,), out_shape=(small, small, jax.Shap...  8.03 us

profile of v3, /device:TPU:1, one launch (start us, length us, event | category | flops | bytes accessed | tf_op | source)
XLA Modules:
  0.0 143.0 jit_solution(6528439084233227622)
XLA Ops:
  0.6 134.3 %shard_map.101 = (bf16[32,1024]{1,0:T(8,128)(2,1)}, bf16[32,1024]{1,0:T(8,128)(2,1)}, bf16[1024,1024]{1,0:T(8,128)(2,1)}, bf16[1024,512]{1,0:T(8,128)(2,1)}, bf1...) custom-call(bf16[32,1024]{1,0:T(8,128)(2,1)} %x_in.1, bf16[32,1024]{1,0:T(8,128)(2,1)} %t_in.1, ...), custom_call_target="tpu_custom_call" | custom-call | flops 6442450944 | bytes 10485760 | tf_op jit(solution)/shard_map/pallas_call | solution.py:326
  135.0 8.0 %shard_map.102 = (bf16[32,1024]{1,0:T(8,128)(2,1)}, bf16[32,1024]{1,0:T(8,128)(2,1)}, f32[1024,512]{1,0:T(8,128)}, f32[1024,512]{1,0:T(8,128)}, f32[512,1024]{1,0:T(8,128)}) custom-call(s32[3,4,8]{2,1,0:T(4,128)} %bitcast.2, bf16[1024,1024]{1,0:T(8,128)(2,1)} %get-tuple-element.11.x, bf16[1024,512]{1,0:T(8,128)(2,1)} %get-tuple-element.12.h, ...), custom_call_target="tpu_custom_call" | custom-call | flops 3221225472 | bytes 13631488 | tf_op jit(solution)/shard_map/pallas_call | solution.py:346

commit v4 on v3

--- a/solution.py
+++ b/solution.py
@@ -284,23 +284,49 @@
         copy.wait()
 
 
-def weight_grads(bm, x, h, e, g, out_in, ig_in, out, ig, gwg, uwg, dwg):
-    p = pl.program_id(0)
-    out[...] = out_in[...]
-    ig[...] = ig_in[...]
-    value = mm(x[...], g[...], TN)
-    for i in range(2):
-        for b in range(8):
-            to = (gwg, uwg)[b // 4]
-            to[pl.ds(i * 128, 128), pl.ds(b % 4 * 128, 128)] = (
-                value[i * 128 : i * 128 + 128, b * 128 : b * 128 + 128]
-                * (bm[b // 4, b % 4, p * 2 + i].astype(F32) * (1.0 / 32.0))
-            )
-    value = mm(h[...], e[...], TN)
-    for a in range(8):
-        dwg[:, pl.ds(a * 128, 128)] = value[:, a * 128 : a * 128 + 128] * (
-            bm[2, p, a].astype(F32) * (1.0 / 32.0)
-        )
+def weight_grads(
+    bm_in, x_in, h_in, e_in, g_in, out_in, ig_in,
+    out, ig, gwg, uwg, dwg,
+    bm, x, h, e, g, gv, uv, dv, in_sems, out_sems,
+):
+    def start(src, dst, sem):
+        copy = pltpu.make_async_copy(src, dst, sem)
+        copy.start()
+        return copy
+
+    loads = [start(src, dst, in_sems.at[i]) for i, (src, dst) in enumerate(
+        ((bm_in, bm), (e_in, e), (h_in, h), (g_in, g), (x_in, x)))]
+    stores = [start(out_in, out, out_sems.at[0]), start(ig_in, ig, out_sems.at[1])]
+
+    def store(src, dst):
+        stores.append(start(src, dst, out_sems.at[len(stores)]))
+
+    for copy in loads[:3]:
+        copy.wait()
+    for p in range(2):
+        at = pl.ds(p * 256, 256)
+        value = mm(h[:, at], e[...], TN)
+        for i in range(2):
+            for a in range(8):
+                dv[pl.ds(p * 256 + i * 128, 128), pl.ds(a * 128, 128)] = value[
+                    i * 128 : i * 128 + 128, a * 128 : a * 128 + 128
+                ] * (bm[2, p * 2 + i, a].astype(F32) * (1.0 / 32.0))
+        store(dv.at[at], dwg.at[at])
+    for copy in loads[3:]:
+        copy.wait()
+    for p in range(4):
+        at = pl.ds(p * 256, 256)
+        value = mm(x[:, at], g[...], TN)
+        for i in range(2):
+            for b in range(8):
+                to = (gv, uv)[b // 4]
+                to[pl.ds(p * 256 + i * 128, 128), pl.ds(b % 4 * 128, 128)] = value[
+                    i * 128 : i * 128 + 128, b * 128 : b * 128 + 128
+                ] * (bm[b // 4, b % 4, p * 2 + i].astype(F32) * (1.0 / 32.0))
+        store(gv.at[at], gwg.at[at])
+        store(uv.at[at], uwg.at[at])
+    for copy in stores:
+        copy.wait()
 
 
 def per_device(student_in, target_delta, gate_weight, up_weight, down_weight, block_mask):
@@ -342,10 +368,8 @@
         ),
         cost_estimate=pl.CostEstimate(flops=6442450944, bytes_accessed=10 << 20, transcendentals=262144),
     )(student_in, target_delta, gate_weight, up_weight, down_weight, block_mask)
-    full = lambda *shape: pl.BlockSpec(shape, lambda p: (0, 0))
     return pl.pallas_call(
         weight_grads,
-        grid=(4,),
         out_shape=(
             small,
             small,
@@ -353,22 +377,13 @@
             jax.ShapeDtypeStruct((D, H), F32),
             jax.ShapeDtypeStruct((H, D), F32),
         ),
-        in_specs=[
-            pl.BlockSpec(memory_space=pltpu.SMEM),
-            pl.BlockSpec((C * T, 256), lambda p: (0, p)),
-            pl.BlockSpec((C * T, 128), lambda p: (0, p)),
-            full(C * T, D),
-            full(C * T, D),
-            full(2 * CHIP, D),
-            full(2 * CHIP, D),
+        in_specs=[anys] * 7,
+        out_specs=(anys,) * 5,
+        scratch_shapes=[
+            pltpu.SMEM((3, 4, 8), jnp.int32), vm((C * T, D), BF), vm((C * T, H), BF), vm((C * T, D), BF),
+            vm((C * T, D), BF), vm((D, H), F32), vm((D, H), F32), vm((H, D), F32),
+            pltpu.SemaphoreType.DMA((5,)), pltpu.SemaphoreType.DMA((12,)),
         ],
-        out_specs=(
-            full(2 * CHIP, D),
-            full(2 * CHIP, D),
-            pl.BlockSpec((256, H), lambda p: (p, 0)),
-            pl.BlockSpec((256, H), lambda p: (p, 0)),
-            pl.BlockSpec((128, D), lambda p: (p, 0)),
-        ),
         compiler_params=pltpu.CompilerParams(vmem_limit_bytes=62 << 20),
         cost_estimate=pl.CostEstimate(flops=3221225472, bytes_accessed=13 << 20, transcendentals=0),
     )(block_mask, x, h, e, g, out, ig)

time: 143 us -> 142 us (level)
    pallas_call x1, Pallas kernels: 8.03 us -> 6.5 us  [per_device(): pl.pallas_call(weight_grads, out_shape=(small, small, jax.ShapeDtypeStruc...]
where the time goes in v4:
time: 142 us; the launch traced here: 141 us
  Pallas kernels  141 us (99%)
    pallas_call x1, Pallas kernels, per_device(): pl.pallas_call(kernel, out_shape=(small, small, square, jax.ShapeDtypeStr...  134 us
    pallas_call x1, Pallas kernels, per_device(): pl.pallas_call(weight_grads, out_shape=(small, small, jax.ShapeDtypeStruc...  6.5 us

profile of v4, /device:TPU:1, one launch (start us, length us, event | category | flops | bytes accessed | tf_op | source)
XLA Modules:
  0.0 141.5 jit_solution(3465837371983544343)
XLA Ops:
  0.6 134.3 %shard_map.101 = (bf16[32,1024]{1,0:T(8,128)(2,1)}, bf16[32,1024]{1,0:T(8,128)(2,1)}, bf16[1024,1024]{1,0:T(8,128)(2,1)}, bf16[1024,512]{1,0:T(8,128)(2,1)}, bf1...) custom-call(bf16[32,1024]{1,0:T(8,128)(2,1)} %x_in.1, bf16[32,1024]{1,0:T(8,128)(2,1)} %t_in.1, ...), custom_call_target="tpu_custom_call" | custom-call | flops 6442450944 | bytes 10485760 | tf_op jit(solution)/shard_map/pallas_call | solution.py:352
  135.0 6.5 %shard_map.102 = (bf16[32,1024]{1,0:T(8,128)(2,1)}, bf16[32,1024]{1,0:T(8,128)(2,1)}, f32[1024,512]{1,0:T(8,128)}, f32[1024,512]{1,0:T(8,128)}, f32[512,1024]{1,0:T(8,128)}) custom-call(s32[3,4,8]{2,1,0:T(4,128)} %bitcast.2, bf16[1024,1024]{1,0:T(8,128)(2,1)} %get-tuple-element.11.x_in, bf16[1024,512]{1,0:T(8,128)(2,1)} %get-tuple-element.12.h_in, ...), custom_call_target="tpu_custom_call" | custom-call | flops 3221225472 | bytes 13631488 | tf_op jit(solution)/shard_map/pallas_call | solution.py:371

commit v5 on v4

--- a/solution.py
+++ b/solution.py
@@ -14,7 +14,7 @@
 Q = 32
 D = 1024
 H = 512
-COPIES = 112
+COPIES = 120
 STEPS = 23
 LAG = 1
 
@@ -125,12 +125,15 @@
     def gather_hid(k, buf):
         own = buf.at[k, rows(block, CHIP), mine]
         zc = send([(own, own, p) for p in zp], buf.at[k, pl.ds(0, 3 * CHIP), mine])
+        xo = send([(own, own, xp[d - 1]) for d in (2, 1, 3)], buf.at[k, pl.ds(0, 3 * CHIP), mine])
         yield
         zc.wait_recv()
         col = buf.at[k, rows(x * XB, XB), mine]
-        xc = send([(col, col, xp[d - 1]) for d in (2, 1, 3)], buf.at[k, pl.ds(0, 3 * XB), mine])
+        rest = [buf.at[k, rows(x * XB + plus(zl, d) * CHIP, CHIP), mine] for d in (1, 2, 3)]
+        xc = send([(r, r, xp[d - 1]) for d in (2, 1, 3) for r in rest], buf.at[k, pl.ds(0, 9 * CHIP), mine])
         s1 = send([(col, col, sib)], col)
         yield
+        xo.wait_recv()
         xc.wait_recv()
         got = [buf.at[k, rows(plus(x, d) * XB, XB), mine] for d in (1, 2, 3)]
         s2 = send([(g, g, sib) for g in got], buf.at[k, pl.ds(0, 3 * XB), mine])
@@ -258,6 +261,16 @@
 
         yield from scatter_hid(k, grads_by_weights, ss8, sl8, of8, xs8, xl8, zs8, zl8)
         isw[k] = scattered(k, of8, zl8).astype(BF)
+
+    def swap_own(held, land):
+        return send([(held.at[2 * (1 - c) + j], land.at[j], sib) for j in range(2)], land)
+
+    def finish(held, land, result, swap):
+        for j in range(2):
+            result[pl.ds(j * CHIP, CHIP), mine] = held[2 * c + j]
+        swap.wait_recv()
+        for j in range(2):
+            result[pl.ds(j * CHIP, CHIP), other] = land[j]
 
     for group in first:
         group.wait_recv()
@@ -270,14 +283,11 @@
                 next(chains[k], None)
         if step == 0:
             mask_weights()
-    swaps = [send([(held.at[2 * (1 - c) + j], land.at[j], sib) for j in range(2)], land)
-             for held, land in ((osw, oland), (isw, iland))]
-    for swap, held, land, result in zip(swaps, (osw, isw), (oland, iland), (out, ig)):
-        for j in range(2):
-            result[pl.ds(j * CHIP, CHIP), mine] = held[2 * c + j]
-        swap.wait_recv()
-        for j in range(2):
-            result[pl.ds(j * CHIP, CHIP), other] = land[j]
+        if step == 16:
+            out_swap = swap_own(osw, oland)
+        if step == 18:
+            finish(osw, oland, out, out_swap)
+    finish(isw, iland, ig, swap_own(isw, iland))
     for group in groups:
         group.wait_send()
     for copy in locals_[8:]:

time: 142 us -> 140 us (0.986)
  Pallas kernels: 141 us -> 139 us
    pallas_call x1, Pallas kernels: 134 us -> 133 us  [per_device(): pl.pallas_call(kernel, out_shape=(small, small, square, jax.ShapeDtypeStr...]
where the time goes in v5:
time: 140 us
  Pallas kernels  139 us (99%)
    pallas_call x1, Pallas kernels, per_device(): pl.pallas_call(kernel, out_shape=(small, small, square, jax.ShapeDtypeStr...  133 us
    pallas_call x1, Pallas kernels, per_device(): pl.pallas_call(weight_grads, out_shape=(small, small, jax.ShapeDtypeStruc...  6.5 us

profile of v5, /device:TPU:1, one launch (start us, length us, event | category | flops | bytes accessed | tf_op | source)
XLA Modules:
  0.0 140.1 jit_solution(3877599468896207510)
XLA Ops:
  0.6 132.8 %shard_map.101 = (bf16[32,1024]{1,0:T(8,128)(2,1)}, bf16[32,1024]{1,0:T(8,128)(2,1)}, bf16[1024,1024]{1,0:T(8,128)(2,1)}, bf16[1024,512]{1,0:T(8,128)(2,1)}, bf1...) custom-call(bf16[32,1024]{1,0:T(8,128)(2,1)} %x_in.1, bf16[32,1024]{1,0:T(8,128)(2,1)} %t_in.1, ...), custom_call_target="tpu_custom_call" | custom-call | flops 6442450944 | bytes 10485760 | tf_op jit(solution)/shard_map/pallas_call | solution.py:362
  133.4 6.5 %shard_map.102 = (bf16[32,1024]{1,0:T(8,128)(2,1)}, bf16[32,1024]{1,0:T(8,128)(2,1)}, f32[1024,512]{1,0:T(8,128)}, f32[1024,512]{1,0:T(8,128)}, f32[512,1024]{1,0:T(8,128)}) custom-call(s32[3,4,8]{2,1,0:T(4,128)} %bitcast.2, bf16[1024,1024]{1,0:T(8,128)(2,1)} %get-tuple-element.11.x_in, bf16[1024,512]{1,0:T(8,128)(2,1)} %get-tuple-element.12.h_in, ...), custom_call_target="tpu_custom_call" | custom-call | flops 3221225472 | bytes 13631488 | tf_op jit(solution)/shard_map/pallas_call | solution.py:381
